TPU v7x, 32 devices: a whole 2x2x4 slice. The times are simulated.
32 devices in a mesh: runs: 2 (over x), area: 16 (over z, y, core).
Axes of the slice: x: 2, y: 2, z: 4, core: 2. Of those that a mesh axis runs over, the one named last changes fastest.
Arguments:
- history: bfloat16 [4, 32, 16384], P(None, 'runs', 'area'), parts along dimension 1, may hold values from 0 to 1
- drive: bfloat16 [32, 16384], P('runs', 'area'), parts along dimension 0, may hold values from -6 to 6
- leak: float32 [32768], P(('runs', 'area')), parts along dimension 0, may hold values from 0.1 to 0.9
- inhibition: float32 [16], P('runs'), parts along dimension 0, may hold values from 0.5 to 4
- section: int32 [16], replicated, may hold values from 0 to 7, never falling along the last dimension, each value on 1 to 6 neighbouring positions
- link_source: int32 [768, 1], P('area'), may hold values from 0 to 15; in each aligned block of 48 rows (0 to 47, 48 to 95, ...) at most 3 rows name the same one
- link_block: int32 [768], P('area'), may hold values from 0 to 3
- link_target: int32 [768], P('area'), may hold values from 0 to 3
- link_delay: int32 [768], P('area'), may hold values from 2 to 4
- remote_weight: bfloat16 [1536, 256, 256], P(('runs', 'area')), parts along dimension 0, may hold values from -0.375 to 0.375
- local_block: int32 [256], P('area'), may hold values from 0 to 3
- local_target: int32 [256], P('area'), may hold values from 0 to 3
- local_delay: int32 [256], P('area'), may hold values from 1 to 4
- local_weight: bfloat16 [512, 256, 256], P(('runs', 'area')), parts along dimension 0, may hold values from -0.375 to 0.375
Outputs:
- rates: bfloat16 [32, 16384], P('runs', 'area'), parts along dimension 0
There are 2 independent parts, one for each index of `runs`. A program takes and returns all parts, laid end to end along the dimension named above; an argument that names none is the same for every part. Nothing has to cross between parts.
Inputs may be any that keep to these rules, and one draw needn't show every extreme that they name: `section`: Nondecreasing; every area covers 1 to 6 consecutive indices, and some area covers exactly 6. `link_source`: among the 48 remote tiles of one index of area, no index of area is named more than 3 times, a bound that some block reaches.
All inputs are finite; a program needn't handle non-finite values.
Results may differ from a plain program's by a relative error of at most 0.005.
Values may be sent and summed in bfloat16 or wider, within the bound.
A program may use at most 128 MiB of HBM per device.

v0:
```python
import jax
import jax.numpy as jnp
from jax import lax
from jax.sharding import PartitionSpec as P

STEPS = 6


def local(
    history,
    drive,
    leak,
    inhibition,
    section,
    link_source,
    link_block,
    link_target,
    link_delay,
    remote_weight,
    local_block,
    local_target,
    local_delay,
    local_weight,
):
    delay_depth, trials, row_width = history.shape
    pop_size = remote_weight.shape[1]
    blocks = row_width // pop_size
    link_count = link_block.shape[0]
    devices = lax.axis_size("area")
    capacity = max(2, (link_count + devices - 1) // devices)
    slot_total = devices * capacity
    area_total = inhibition.shape[0]
    state_rows = (
        history.reshape(delay_depth, trials, blocks, pop_size)
        .transpose(0, 2, 1, 3)
        .reshape(delay_depth * blocks, trials, pop_size)
    )
    source = link_source[:, 0]
    positions = jnp.arange(link_count, dtype=jnp.int32)
    earlier = (source[:, None] == source[None, :]) & (positions[None, :] < positions[:, None])
    slot_rank = jnp.sum(earlier.astype(jnp.int32), axis=1)
    slot_index = source * capacity + slot_rank
    slot_table = slot_index[:, None] == jnp.arange(slot_total, dtype=jnp.int32)[None, :]
    slot_used = jnp.any(slot_table, axis=0)
    want_block = jnp.sum(jnp.where(slot_table, link_block[:, None], 0), axis=0)
    want_delay = jnp.where(
        slot_used, jnp.sum(jnp.where(slot_table, link_delay[:, None], 0), axis=0), delay_depth
    )
    asked_block, asked_delay = (
        lax.all_to_all(
            want_block.reshape(devices, capacity), "area", split_axis=0, concat_axis=0, tiled=True
        ),
        lax.all_to_all(
            want_delay.reshape(devices, capacity), "area", split_axis=0, concat_axis=0, tiled=True
        ),
    )
    asked_block = asked_block.reshape(slot_total)
    asked_delay = asked_delay.reshape(slot_total)
    target_onehot = (link_target[None, :] == jnp.arange(blocks, dtype=jnp.int32)[:, None]).astype(
        jnp.float32
    )
    local_onehot = (local_target[None, :] == jnp.arange(blocks, dtype=jnp.int32)[:, None]).astype(
        jnp.float32
    )
    local_index = (local_delay - 1) * blocks + local_block
    leak_rows = leak.reshape(blocks, pop_size)[:, None, :]
    drive_blocks = drive.astype(jnp.float32).reshape(trials, blocks, pop_size).transpose(1, 0, 2)
    my_index = lax.axis_index("area")
    my_area = lax.dynamic_slice_in_dim(section, my_index, 1, 0)[0]
    area_mask = jnp.arange(area_total, dtype=jnp.int32) == my_area
    area_count = jnp.sum((section == my_area).astype(jnp.float32)) * row_width
    inhibit = jnp.sum(jnp.where(area_mask, inhibition, 0.0))
    fresh = state_rows[:blocks]
    for step_index in range(STEPS):
        outgoing = jnp.take(state_rows, (asked_delay - 1) * blocks + asked_block, axis=0).reshape(
            devices, capacity, trials, pop_size
        )
        received = lax.all_to_all(
            outgoing, "area", split_axis=0, concat_axis=0, tiled=True
        ).reshape(slot_total, trials, pop_size)
        remote_in = jnp.take(received, slot_index, axis=0)
        previous = state_rows[:blocks].astype(jnp.float32)
        own_sum = jnp.sum(previous, axis=(0, 2))
        area_table = jnp.where(area_mask[:, None], own_sum[None, :], 0.0)
        summed = lax.psum(area_table, "area")
        total_mine = jnp.sum(jnp.where(area_mask[:, None], summed, 0.0), axis=0)
        mean_now = total_mine / area_count
        local_in = jnp.take(state_rows, local_index, axis=0)
        local_terms = jnp.einsum(
            "ltp,lpq->ltq", local_in, local_weight, preferred_element_type=jnp.float32
        )
        remote_terms = jnp.einsum(
            "ltp,lpq->ltq", remote_in, remote_weight, preferred_element_type=jnp.float32
        )
        current = jnp.einsum(
            "bl,ltq->btq", target_onehot, remote_terms, precision=lax.Precision.HIGHEST
        )
        current = current + jnp.einsum(
            "bl,ltq->btq", local_onehot, local_terms, precision=lax.Precision.HIGHEST
        )
        driven = jax.nn.sigmoid(current + drive_blocks - inhibit * mean_now[None, :, None])
        fresh = ((1.0 - leak_rows) * previous + leak_rows * driven).astype(jnp.bfloat16)
        state_rows = jnp.concatenate([fresh, state_rows[:-blocks]], axis=0)
    return fresh.transpose(1, 0, 2).reshape(trials, row_width)


def solution(mesh):
    placed = (
        P(None, "runs", "area"),
        P("runs", "area"),
        P(("runs", "area")),
        P("runs"),
        P(),
        P("area", None),
        P("area"),
        P("area"),
        P("area"),
        P(("runs", "area"), None, None),
        P("area"),
        P("area"),
        P("area"),
        P(("runs", "area"), None, None),
    )
    return jax.shard_map(
        local, mesh=mesh, in_specs=placed, out_specs=P("runs", "area"), check_vma=False
    )
```

profile of v0, /device:TPU:0, one launch (start us, length us, event | category | flops | bytes accessed | tf_op | source)
XLA Modules:
  0.0 361.1 jit_solution(18329687779567038272)
XLA Ops:
  3.1 7.4 %all-to-all-start.1 = ((s32[16,1,3]{2,1,0:T(1,128)}), s32[16,1,3]{2,1,0:T(1,128)S(1)}, u32[]{:S(2)}, u32[]{:S(2)}) async-start(s32[16,1,3]{2,1,0:T(1,128)} %bitcast.6), calls=%async_computation.1 | async-start | bytes 16384 | tf_op jit(solution)/shard_map/all_to_all | solution.py:50
  12.3 1.3 dynamic_slice.3
  14.3 2.0 select_reduce_fusion.8
  17.9 33.8 %psum.42 = f32[8,16]{1,0:T(8,128)S(1)} all-reduce(f32[8,16]{1,0:T(8,128)S(1)} %broadcast_select_fusion.11), channel_id=1, replica_groups=mesh['runs'=2,'area'=16] {'area'}, use_global_device_ids=true, to_apply=%region_7.11 | all-reduce | flops 128 | bytes 1024 | tf_op jit(solution)/shard_map/psum | solution.py:85
  51.8 1.9 fusion.129
  54.4 3.5 all-to-all-start
  59.9 4.4 %all-to-all-done = s32[16,1,3]{2,1,0:T(1,128)S(1)} async-done(((s32[16,1,3]{2,1,0:T(1,128)}), s32[16,1,3]{2,1,0:T(1,128)S(1)}, u32[]{:S(2)}, u32[]{:S(2)}) %all-to-all-start) | async-done | bytes 224 | tf_op jit(solution)/shard_map/all_to_all | solution.py:53
  65.9 3.6 all-to-all-start.2
  70.6 1.0 fusion.88
  71.6 10.1 %all-to-all-done.2 = bf16[16,3,16,256]{3,2,1,0:T(8,128)(2,1)S(1)} async-done(((bf16[16,3,16,256]{3,2,1,0:T(8,128)(2,1)}), bf16[16,3,16,256]{3,2,1,0:T(8,128)(2,1)S(1)}, u32[]{:S(2)}, u32[]{:S(2)}) %all-to-all-start.2) | async-done | bytes 393248 | tf_op jit(solution)/shard_map/all_to_all | solution.py:78
  82.2 3.8 %fusion.70 = f32[48,16,256]{2,1,0:T(8,128)S(1)} fusion(bf16[48,256,256]{2,1,0:T(8,128)(2,1)} %param.29, bf16[48,16,256]{2,1,0:T(8,128)(2,1)S(1)} %gather_fusion.1, pred[48]{0:T(512)(128)(4,1)S(1)} %get-tuple-element.10), kind=kOutput, calls=%fused_computation.94 | convolution fusion | flops 100859904 | bytes 7471152 | tf_op jit(solution)/shard_map/ltp,lpq->ltq/dot_general | solution.py:92
  86.0 1.0 convert_reduce_fusion.4
  88.3 31.4 %psum.43 = f32[8,16]{1,0:T(8,128)S(1)} all-reduce(f32[8,16]{1,0:T(8,128)S(1)} %broadcast_select_fusion.10), channel_id=1, replica_groups=mesh['runs'=2,'area'=16] {'area'}, use_global_device_ids=true, to_apply=%region_11.15 | all-reduce | flops 128 | bytes 1024 | tf_op jit(solution)/shard_map/psum | solution.py:85
  120.7 3.6 all-to-all-start.3
  125.7 10.7 %all-to-all-done.3 = bf16[16,3,16,256]{3,2,1,0:T(8,128)(2,1)S(1)} async-done(((bf16[16,3,16,256]{3,2,1,0:T(8,128)(2,1)}), bf16[16,3,16,256]{3,2,1,0:T(8,128)(2,1)S(1)}, u32[]{:S(2)}, u32[]{:S(2)}) %all-to-all-start.3) | async-done | bytes 393248 | tf_op jit(solution)/shard_map/all_to_all | solution.py:78
  137.0 3.7 %fusion.68 = f32[48,16,256]{2,1,0:T(8,128)S(1)} fusion(bf16[48,256,256]{2,1,0:T(8,128)(2,1)} %param.29, bf16[48,16,256]{2,1,0:T(8,128)(2,1)S(1)} %gather_fusion.4, pred[48]{0:T(512)(128)(4,1)S(1)} %get-tuple-element.10), kind=kOutput, calls=%fused_computation.92 | convolution fusion | flops 100859904 | bytes 7471152 | tf_op jit(solution)/shard_map/ltp,lpq->ltq/dot_general | solution.py:92
  143.0 31.4 %psum.44 = f32[8,16]{1,0:T(8,128)S(1)} all-reduce(f32[8,16]{1,0:T(8,128)S(1)} %broadcast_select_fusion.9), channel_id=1, replica_groups=mesh['runs'=2,'area'=16] {'area'}, use_global_device_ids=true, to_apply=%region_14.18 | all-reduce | flops 128 | bytes 1024 | tf_op jit(solution)/shard_map/psum | solution.py:85
  175.4 3.6 all-to-all-start.4
  180.4 10.7 %all-to-all-done.4 = bf16[16,3,16,256]{3,2,1,0:T(8,128)(2,1)S(1)} async-done(((bf16[16,3,16,256]{3,2,1,0:T(8,128)(2,1)}), bf16[16,3,16,256]{3,2,1,0:T(8,128)(2,1)S(1)}, u32[]{:S(2)}, u32[]{:S(2)}) %all-to-all-start.4) | async-done | bytes 393248 | tf_op jit(solution)/shard_map/all_to_all | solution.py:78
  191.7 3.7 %fusion.66 = f32[48,16,256]{2,1,0:T(8,128)S(1)} fusion(bf16[48,256,256]{2,1,0:T(8,128)(2,1)} %param.29, bf16[48,16,256]{2,1,0:T(8,128)(2,1)S(1)} %gather_fusion.7, pred[48]{0:T(512)(128)(4,1)S(1)} %get-tuple-element.10), kind=kOutput, calls=%fused_computation.90 | convolution fusion | flops 100859904 | bytes 7471152 | tf_op jit(solution)/shard_map/ltp,lpq->ltq/dot_general | solution.py:92
  197.8 31.4 %psum.45 = f32[8,16]{1,0:T(8,128)S(1)} all-reduce(f32[8,16]{1,0:T(8,128)S(1)} %broadcast_select_fusion.8), channel_id=1, replica_groups=mesh['runs'=2,'area'=16] {'area'}, use_global_device_ids=true, to_apply=%region_17.21 | all-reduce | flops 128 | bytes 1024 | tf_op jit(solution)/shard_map/psum | solution.py:85
  230.2 3.7 %all-to-all-start.5 = ((bf16[16,3,16,256]{3,2,1,0:T(8,128)(2,1)}), bf16[16,3,16,256]{3,2,1,0:T(8,128)(2,1)S(1)}, u32[]{:S(2)}, u32[]{:S(2)}) async-start(bf16[16,3,16,256]{3,2,1,0:T(8,128)(2,1)} %bitcast.18), calls=%async_computation.5 | async-start | bytes 786432 | tf_op jit(solution)/shard_map/all_to_all | solution.py:78
  235.3 10.5 %all-to-all-done.5 = bf16[16,3,16,256]{3,2,1,0:T(8,128)(2,1)S(1)} async-done(((bf16[16,3,16,256]{3,2,1,0:T(8,128)(2,1)}), bf16[16,3,16,256]{3,2,1,0:T(8,128)(2,1)S(1)}, u32[]{:S(2)}, u32[]{:S(2)}) %all-to-all-start.5) | async-done | bytes 393248 | tf_op jit(solution)/shard_map/all_to_all | solution.py:78
  246.5 3.7 %fusion.64 = f32[48,16,256]{2,1,0:T(8,128)S(1)} fusion(bf16[48,256,256]{2,1,0:T(8,128)(2,1)} %param.29, bf16[48,16,256]{2,1,0:T(8,128)(2,1)S(1)} %gather_fusion.10, pred[48]{0:T(512)(128)(4,1)S(1)} %get-tuple-element.10), kind=kOutput, calls=%fused_computation.88 | convolution fusion | flops 100859904 | bytes 7471152 | tf_op jit(solution)/shard_map/ltp,lpq->ltq/dot_general | solution.py:92
  252.5 31.4 %psum.46 = f32[8,16]{1,0:T(8,128)S(1)} all-reduce(f32[8,16]{1,0:T(8,128)S(1)} %broadcast_select_fusion.7), channel_id=1, replica_groups=mesh['runs'=2,'area'=16] {'area'}, use_global_device_ids=true, to_apply=%region_20.24 | all-reduce | flops 128 | bytes 1024 | tf_op jit(solution)/shard_map/psum | solution.py:85
  284.9 3.6 all-to-all-start.6
  289.9 10.7 %all-to-all-done.6 = bf16[16,3,16,256]{3,2,1,0:T(8,128)(2,1)S(1)} async-done(((bf16[16,3,16,256]{3,2,1,0:T(8,128)(2,1)}), bf16[16,3,16,256]{3,2,1,0:T(8,128)(2,1)S(1)}, u32[]{:S(2)}, u32[]{:S(2)}) %all-to-all-start.6) | async-done | bytes 393248 | tf_op jit(solution)/shard_map/all_to_all | solution.py:78
  301.2 3.7 %fusion.62 = f32[48,16,256]{2,1,0:T(8,128)S(1)} fusion(bf16[48,256,256]{2,1,0:T(8,128)(2,1)} %param.29, bf16[48,16,256]{2,1,0:T(8,128)(2,1)S(1)} %gather_fusion.13, pred[48]{0:T(512)(128)(4,1)S(1)} %get-tuple-element.10), kind=kOutput, calls=%fused_computation.86 | convolution fusion | flops 100859904 | bytes 7471152 | tf_op jit(solution)/shard_map/ltp,lpq->ltq/dot_general | solution.py:92
  307.2 31.4 %psum.47 = f32[8,16]{1,0:T(8,128)S(1)} all-reduce(f32[8,16]{1,0:T(8,128)S(1)} %broadcast_select_fusion.6), channel_id=1, replica_groups=mesh['runs'=2,'area'=16] {'area'}, use_global_device_ids=true, to_apply=%region_23.27 | all-reduce | flops 128 | bytes 1024 | tf_op jit(solution)/shard_map/psum | solution.py:85
  339.6 3.6 all-to-all-start.7
  344.6 10.7 %all-to-all-done.7 = bf16[16,3,16,256]{3,2,1,0:T(8,128)(2,1)S(1)} async-done(((bf16[16,3,16,256]{3,2,1,0:T(8,128)(2,1)}), bf16[16,3,16,256]{3,2,1,0:T(8,128)(2,1)S(1)}, u32[]{:S(2)}, u32[]{:S(2)}) %all-to-all-start.7) | async-done | bytes 393248 | tf_op jit(solution)/shard_map/all_to_all | solution.py:78
  355.9 3.7 %fusion.60 = f32[48,16,256]{2,1,0:T(8,128)S(1)} fusion(bf16[48,256,256]{2,1,0:T(8,128)(2,1)} %param.29, bf16[48,16,256]{2,1,0:T(8,128)(2,1)S(1)} %gather_fusion.16, pred[48]{0:T(512)(128)(4,1)S(1)} %get-tuple-element.10), kind=kOutput, calls=%fused_computation.84 | convolution fusion | flops 100859904 | bytes 7471152 | tf_op jit(solution)/shard_map/ltp,lpq->ltq/dot_general | solution.py:92
  (107 shorter events, 38.9 us)
Async XLA Ops:
  0.0 70.1 %copy-start = (bf16[16,256,256]{2,1,0:T(8,128)(2,1)S(1)}, bf16[16,256,256]{2,1,0:T(8,128)(2,1)}, u32[]{:S(2)}) copy-start(bf16[16,256,256]{2,1,0:T(8,128)(2,1)} %param.33) | copy-start | bytes 6291460
  3.1 51.3 %all-to-all-start.1 = ((s32[16,1,3]{2,1,0:T(1,128)}), s32[16,1,3]{2,1,0:T(1,128)S(1)}, u32[]{:S(2)}, u32[]{:S(2)}) async-start(s32[16,1,3]{2,1,0:T(1,128)} %bitcast.6), calls=%async_computation.1 | async-start | bytes 16384 | tf_op jit(solution)/shard_map/all_to_all | solution.py:50
  54.4 9.9 %all-to-all-start = ((s32[16,1,3]{2,1,0:T(1,128)}), s32[16,1,3]{2,1,0:T(1,128)S(1)}, u32[]{:S(2)}, u32[]{:S(2)}) async-start(s32[16,1,3]{2,1,0:T(1,128)} %bitcast.5), calls=%async_computation | async-start | bytes 16384 | tf_op jit(solution)/shard_map/all_to_all | solution.py:53
  65.1 20.9 %copy-start.2 = (s32[48]{0:T(128)S(1)}, s32[48]{0:T(128)}, u32[]{:S(2)}) copy-start(s32[48]{0:T(128)} %param.27) | copy-start | bytes 580
  65.9 15.7 %all-to-all-start.2 = ((bf16[16,3,16,256]{3,2,1,0:T(8,128)(2,1)}), bf16[16,3,16,256]{3,2,1,0:T(8,128)(2,1)S(1)}, u32[]{:S(2)}, u32[]{:S(2)}) async-start(bf16[16,3,16,256]{3,2,1,0:T(8,128)(2,1)} %bitcast.8), calls=%async_computation.2 | async-start | bytes 786432 | tf_op jit(solution)/shard_map/all_to_all | solution.py:78
  82.2 43.1 %copy-start.1 = (s32[16]{0:T(128)S(1)}, s32[16]{0:T(128)}, u32[]{:S(2)}) copy-start(s32[16]{0:T(128)} %param.31) | copy-start | bytes 196
  120.7 15.7 %all-to-all-start.3 = ((bf16[16,3,16,256]{3,2,1,0:T(8,128)(2,1)}), bf16[16,3,16,256]{3,2,1,0:T(8,128)(2,1)S(1)}, u32[]{:S(2)}, u32[]{:S(2)}) async-start(bf16[16,3,16,256]{3,2,1,0:T(8,128)(2,1)} %bitcast.14), calls=%async_computation.3 | async-start | bytes 786432 | tf_op jit(solution)/shard_map/all_to_all | solution.py:78
  175.4 15.7 %all-to-all-start.4 = ((bf16[16,3,16,256]{3,2,1,0:T(8,128)(2,1)}), bf16[16,3,16,256]{3,2,1,0:T(8,128)(2,1)S(1)}, u32[]{:S(2)}, u32[]{:S(2)}) async-start(bf16[16,3,16,256]{3,2,1,0:T(8,128)(2,1)} %bitcast.16), calls=%async_computation.4 | async-start | bytes 786432 | tf_op jit(solution)/shard_map/all_to_all | solution.py:78
  230.2 15.7 %all-to-all-start.5 = ((bf16[16,3,16,256]{3,2,1,0:T(8,128)(2,1)}), bf16[16,3,16,256]{3,2,1,0:T(8,128)(2,1)S(1)}, u32[]{:S(2)}, u32[]{:S(2)}) async-start(bf16[16,3,16,256]{3,2,1,0:T(8,128)(2,1)} %bitcast.18), calls=%async_computation.5 | async-start | bytes 786432 | tf_op jit(solution)/shard_map/all_to_all | solution.py:78
  284.9 15.7 %all-to-all-start.6 = ((bf16[16,3,16,256]{3,2,1,0:T(8,128)(2,1)}), bf16[16,3,16,256]{3,2,1,0:T(8,128)(2,1)S(1)}, u32[]{:S(2)}, u32[]{:S(2)}) async-start(bf16[16,3,16,256]{3,2,1,0:T(8,128)(2,1)} %bitcast.20), calls=%async_computation.6 | async-start | bytes 786432 | tf_op jit(solution)/shard_map/all_to_all | solution.py:78
  339.6 15.7 %all-to-all-start.7 = ((bf16[16,3,16,256]{3,2,1,0:T(8,128)(2,1)}), bf16[16,3,16,256]{3,2,1,0:T(8,128)(2,1)S(1)}, u32[]{:S(2)}, u32[]{:S(2)}) async-start(bf16[16,3,16,256]{3,2,1,0:T(8,128)(2,1)} %bitcast.22), calls=%async_computation.7 | async-start | bytes 786432 | tf_op jit(solution)/shard_map/all_to_all | solution.py:78
where the time goes:
time: 363 us; the launch traced here: 361 us
  blocking collectives  191 us (53%)
  waiting for transfers between devices  67.9 us (19%)
  matrix products  33.8 us (9%)
  starting transfers between devices  32.4 us (9%)
  other arithmetic  18.7 us (5%)
  local copies, waits for them, and re-layouts  16.2 us (4%)
    psum x6, blocking collectives, local(): summed = lax.psum(area_table, 'area')  191 us
    all_to_all x6, waiting for transfers between devices, local(): lax.all_to_all(outgoing, 'area', split_axis=0, concat_axis=0, tiled=True)  63.5 us
    dot_general x6, matrix products, local(): jnp.einsum('ltp,lpq->ltq', remote_in, remote_weight, preferred_element_ty...  22.5 us
    all_to_all x6, starting transfers between devices, local(): lax.all_to_all(outgoing, 'area', split_axis=0, concat_axis=0, tiled=True)  21.5 us
    all_to_all x1, starting transfers between devices, local(): lax.all_to_all(want_block.reshape(devices, capacity), 'area', split_axis=...  7.39 us
  transfers between devices with their start and end apart: 8, of which 7 were waited for; matrix products, arithmetic and copies ran while one was open for 6% of the time, Pallas kernels for 0%

commit v1 on v0

--- a/solution.py
+++ b/solution.py
@@ -82,7 +82,7 @@
         previous = state_rows[:blocks].astype(jnp.float32)
         own_sum = jnp.sum(previous, axis=(0, 2))
         area_table = jnp.where(area_mask[:, None], own_sum[None, :], 0.0)
-        summed = lax.psum(area_table, "area")
+        summed = jnp.sum(lax.all_gather(area_table, "area"), axis=0)
         total_mine = jnp.sum(jnp.where(area_mask[:, None], summed, 0.0), axis=0)
         mean_now = total_mine / area_count
         local_in = jnp.take(state_rows, local_index, axis=0)

time: 363 us -> 290 us (0.80)
  blocking collectives: 191 us -> 118 us
    psum x6 -> x0, blocking collectives: 191 us -> none  [local(): summed = lax.psum(area_table, 'area')]
    all_gather x0 -> x6, blocking collectives: none -> 118 us  [local(): summed = jnp.sum(lax.all_gather(area_table, 'area'), axis=0)]
  transfers between devices with their start and end apart: 8 -> 8, of which waited for: 7 -> 7; matrix products, arithmetic and copies ran while one was open for 6% -> 7% of each run, Pallas kernels for 0% -> 0%
where the time goes in v1:
time: 290 us; the launch traced here: 289 us
  blocking collectives  118 us (41%)
  waiting for transfers between devices  68.6 us (24%)
  matrix products  33.1 us (11%)
  starting transfers between devices  32.4 us (11%)
  other arithmetic  18.9 us (7%)
  local copies, waits for them, and re-layouts  16.2 us (6%)
    all_gather x6, blocking collectives, local(): summed = jnp.sum(lax.all_gather(area_table, 'area'), axis=0)  118 us
    all_to_all x6, waiting for transfers between devices, local(): lax.all_to_all(outgoing, 'area', split_axis=0, concat_axis=0, tiled=True)  64.2 us
    dot_general x6, matrix products, local(): jnp.einsum('ltp,lpq->ltq', remote_in, remote_weight, preferred_element_ty...  22.5 us
    all_to_all x6, starting transfers between devices, local(): lax.all_to_all(outgoing, 'area', split_axis=0, concat_axis=0, tiled=True)  21.5 us
    all_to_all x1, starting transfers between devices, local(): lax.all_to_all(want_block.reshape(devices, capacity), 'area', split_axis=...  7.39 us
    dot_general x6, matrix products, local(): jnp.einsum('bl,ltq->btq', target_onehot, remote_terms, precision=lax.Prec...  5.92 us
  transfers between devices with their start and end apart: 8, of which 7 were waited for; matrix products, arithmetic and copies ran while one was open for 7% of the time, Pallas kernels for 0%

profile of v1, /device:TPU:0, one launch (start us, length us, event | category | flops | bytes accessed | tf_op | source)
XLA Modules:
  0.0 288.7 jit_solution(14914656625586996096)
XLA Ops:
  3.1 7.4 %all-to-all-start.1 = ((s32[16,1,3]{2,1,0:T(1,128)}), s32[16,1,3]{2,1,0:T(1,128)S(1)}, u32[]{:S(2)}, u32[]{:S(2)}) async-start(s32[16,1,3]{2,1,0:T(1,128)} %bitcast.6), calls=%async_computation.1 | async-start | bytes 16384 | tf_op jit(solution)/shard_map/all_to_all | solution.py:50
  12.3 1.3 dynamic_slice.3
  14.3 2.0 select_reduce_fusion.8
  17.9 21.9 %all_gather.24 = f32[16,8,16]{2,1,0:T(8,128)S(1)} all-gather(f32[1,8,16]{2,1,0:T(8,128)S(1)} %broadcast_select_fusion.11), channel_id=1, replica_groups=mesh['runs'=2,'area'=16] {'area'}, dimensions={0}, use_global_device_ids=true | all-gather | bytes 8704 | tf_op jit(solution)/shard_map/all_gather | solution.py:85
  39.9 1.9 fusion.129
  42.5 3.5 %all-to-all-start = ((s32[16,1,3]{2,1,0:T(1,128)}), s32[16,1,3]{2,1,0:T(1,128)S(1)}, u32[]{:S(2)}, u32[]{:S(2)}) async-start(s32[16,1,3]{2,1,0:T(1,128)} %bitcast.5), calls=%async_computation | async-start | bytes 16384 | tf_op jit(solution)/shard_map/all_to_all | solution.py:53
  47.9 4.4 %all-to-all-done = s32[16,1,3]{2,1,0:T(1,128)S(1)} async-done(((s32[16,1,3]{2,1,0:T(1,128)}), s32[16,1,3]{2,1,0:T(1,128)S(1)}, u32[]{:S(2)}, u32[]{:S(2)}) %all-to-all-start) | async-done | bytes 224 | tf_op jit(solution)/shard_map/all_to_all | solution.py:53
  54.0 3.6 %all-to-all-start.2 = ((bf16[16,3,16,256]{3,2,1,0:T(8,128)(2,1)}), bf16[16,3,16,256]{3,2,1,0:T(8,128)(2,1)S(1)}, u32[]{:S(2)}, u32[]{:S(2)}) async-start(bf16[16,3,16,256]{3,2,1,0:T(8,128)(2,1)} %bitcast.8), calls=%async_computation.2 | async-start | bytes 786432 | tf_op jit(solution)/shard_map/all_to_all | solution.py:78
  59.0 10.7 %all-to-all-done.2 = bf16[16,3,16,256]{3,2,1,0:T(8,128)(2,1)S(1)} async-done(((bf16[16,3,16,256]{3,2,1,0:T(8,128)(2,1)}), bf16[16,3,16,256]{3,2,1,0:T(8,128)(2,1)S(1)}, u32[]{:S(2)}, u32[]{:S(2)}) %all-to-all-start.2) | async-done | bytes 393248 | tf_op jit(solution)/shard_map/all_to_all | solution.py:78
  70.3 3.7 %fusion.70 = f32[48,16,256]{2,1,0:T(8,128)S(1)} fusion(bf16[48,256,256]{2,1,0:T(8,128)(2,1)} %param.29, bf16[48,16,256]{2,1,0:T(8,128)(2,1)S(1)} %gather_fusion.1, pred[48]{0:T(512)(128)(4,1)S(1)} %get-tuple-element.10), kind=kOutput, calls=%fused_computation.94 | convolution fusion | flops 100859904 | bytes 7471152 | tf_op jit(solution)/shard_map/ltp,lpq->ltq/dot_general | solution.py:92
  74.0 1.0 convert_reduce_fusion.4
  76.3 19.3 %all_gather.25 = f32[16,8,16]{2,1,0:T(8,128)S(1)} all-gather(f32[1,8,16]{2,1,0:T(8,128)S(1)} %broadcast_select_fusion.10), channel_id=1, replica_groups=mesh['runs'=2,'area'=16] {'area'}, dimensions={0}, use_global_device_ids=true | all-gather | bytes 8704 | tf_op jit(solution)/shard_map/all_gather | solution.py:85
  96.6 3.6 %all-to-all-start.3 = ((bf16[16,3,16,256]{3,2,1,0:T(8,128)(2,1)}), bf16[16,3,16,256]{3,2,1,0:T(8,128)(2,1)S(1)}, u32[]{:S(2)}, u32[]{:S(2)}) async-start(bf16[16,3,16,256]{3,2,1,0:T(8,128)(2,1)} %bitcast.14), calls=%async_computation.3 | async-start | bytes 786432 | tf_op jit(solution)/shard_map/all_to_all | solution.py:78
  101.6 10.7 %all-to-all-done.3 = bf16[16,3,16,256]{3,2,1,0:T(8,128)(2,1)S(1)} async-done(((bf16[16,3,16,256]{3,2,1,0:T(8,128)(2,1)}), bf16[16,3,16,256]{3,2,1,0:T(8,128)(2,1)S(1)}, u32[]{:S(2)}, u32[]{:S(2)}) %all-to-all-start.3) | async-done | bytes 393248 | tf_op jit(solution)/shard_map/all_to_all | solution.py:78
  112.9 3.7 %fusion.68 = f32[48,16,256]{2,1,0:T(8,128)S(1)} fusion(bf16[48,256,256]{2,1,0:T(8,128)(2,1)} %param.29, bf16[48,16,256]{2,1,0:T(8,128)(2,1)S(1)} %gather_fusion.4, pred[48]{0:T(512)(128)(4,1)S(1)} %get-tuple-element.10), kind=kOutput, calls=%fused_computation.92 | convolution fusion | flops 100859904 | bytes 7471152 | tf_op jit(solution)/shard_map/ltp,lpq->ltq/dot_general | solution.py:92
  119.0 19.3 %all_gather.26 = f32[16,8,16]{2,1,0:T(8,128)S(1)} all-gather(f32[1,8,16]{2,1,0:T(8,128)S(1)} %broadcast_select_fusion.9), channel_id=1, replica_groups=mesh['runs'=2,'area'=16] {'area'}, dimensions={0}, use_global_device_ids=true | all-gather | bytes 8704 | tf_op jit(solution)/shard_map/all_gather | solution.py:85
  139.3 3.6 %all-to-all-start.4 = ((bf16[16,3,16,256]{3,2,1,0:T(8,128)(2,1)}), bf16[16,3,16,256]{3,2,1,0:T(8,128)(2,1)S(1)}, u32[]{:S(2)}, u32[]{:S(2)}) async-start(bf16[16,3,16,256]{3,2,1,0:T(8,128)(2,1)} %bitcast.16), calls=%async_computation.4 | async-start | bytes 786432 | tf_op jit(solution)/shard_map/all_to_all | solution.py:78
  144.3 10.7 %all-to-all-done.4 = bf16[16,3,16,256]{3,2,1,0:T(8,128)(2,1)S(1)} async-done(((bf16[16,3,16,256]{3,2,1,0:T(8,128)(2,1)}), bf16[16,3,16,256]{3,2,1,0:T(8,128)(2,1)S(1)}, u32[]{:S(2)}, u32[]{:S(2)}) %all-to-all-start.4) | async-done | bytes 393248 | tf_op jit(solution)/shard_map/all_to_all | solution.py:78
  155.6 3.7 %fusion.66 = f32[48,16,256]{2,1,0:T(8,128)S(1)} fusion(bf16[48,256,256]{2,1,0:T(8,128)(2,1)} %param.29, bf16[48,16,256]{2,1,0:T(8,128)(2,1)S(1)} %gather_fusion.7, pred[48]{0:T(512)(128)(4,1)S(1)} %get-tuple-element.10), kind=kOutput, calls=%fused_computation.90 | convolution fusion | flops 100859904 | bytes 7471152 | tf_op jit(solution)/shard_map/ltp,lpq->ltq/dot_general | solution.py:92
  161.6 19.3 %all_gather.27 = f32[16,8,16]{2,1,0:T(8,128)S(1)} all-gather(f32[1,8,16]{2,1,0:T(8,128)S(1)} %broadcast_select_fusion.8), channel_id=1, replica_groups=mesh['runs'=2,'area'=16] {'area'}, dimensions={0}, use_global_device_ids=true | all-gather | bytes 8704 | tf_op jit(solution)/shard_map/all_gather | solution.py:85
  181.9 3.7 %all-to-all-start.5 = ((bf16[16,3,16,256]{3,2,1,0:T(8,128)(2,1)}), bf16[16,3,16,256]{3,2,1,0:T(8,128)(2,1)S(1)}, u32[]{:S(2)}, u32[]{:S(2)}) async-start(bf16[16,3,16,256]{3,2,1,0:T(8,128)(2,1)} %bitcast.18), calls=%async_computation.5 | async-start | bytes 786432 | tf_op jit(solution)/shard_map/all_to_all | solution.py:78
  187.1 10.5 %all-to-all-done.5 = bf16[16,3,16,256]{3,2,1,0:T(8,128)(2,1)S(1)} async-done(((bf16[16,3,16,256]{3,2,1,0:T(8,128)(2,1)}), bf16[16,3,16,256]{3,2,1,0:T(8,128)(2,1)S(1)}, u32[]{:S(2)}, u32[]{:S(2)}) %all-to-all-start.5) | async-done | bytes 393248 | tf_op jit(solution)/shard_map/all_to_all | solution.py:78
  198.2 3.7 %fusion.64 = f32[48,16,256]{2,1,0:T(8,128)S(1)} fusion(bf16[48,256,256]{2,1,0:T(8,128)(2,1)} %param.29, bf16[48,16,256]{2,1,0:T(8,128)(2,1)S(1)} %gather_fusion.10, pred[48]{0:T(512)(128)(4,1)S(1)} %get-tuple-element.10), kind=kOutput, calls=%fused_computation.88 | convolution fusion | flops 100859904 | bytes 7471152 | tf_op jit(solution)/shard_map/ltp,lpq->ltq/dot_general | solution.py:92
  204.3 19.4 %all_gather.28 = f32[16,8,16]{2,1,0:T(8,128)S(1)} all-gather(f32[1,8,16]{2,1,0:T(8,128)S(1)} %broadcast_select_fusion.7), channel_id=1, replica_groups=mesh['runs'=2,'area'=16] {'area'}, dimensions={0}, use_global_device_ids=true | all-gather | bytes 8704 | tf_op jit(solution)/shard_map/all_gather | solution.py:85
  224.6 3.6 %all-to-all-start.6 = ((bf16[16,3,16,256]{3,2,1,0:T(8,128)(2,1)}), bf16[16,3,16,256]{3,2,1,0:T(8,128)(2,1)S(1)}, u32[]{:S(2)}, u32[]{:S(2)}) async-start(bf16[16,3,16,256]{3,2,1,0:T(8,128)(2,1)} %bitcast.20), calls=%async_computation.6 | async-start | bytes 786432 | tf_op jit(solution)/shard_map/all_to_all | solution.py:78
  229.6 10.7 %all-to-all-done.6 = bf16[16,3,16,256]{3,2,1,0:T(8,128)(2,1)S(1)} async-done(((bf16[16,3,16,256]{3,2,1,0:T(8,128)(2,1)}), bf16[16,3,16,256]{3,2,1,0:T(8,128)(2,1)S(1)}, u32[]{:S(2)}, u32[]{:S(2)}) %all-to-all-start.6) | async-done | bytes 393248 | tf_op jit(solution)/shard_map/all_to_all | solution.py:78
  240.9 3.7 %fusion.62 = f32[48,16,256]{2,1,0:T(8,128)S(1)} fusion(bf16[48,256,256]{2,1,0:T(8,128)(2,1)} %param.29, bf16[48,16,256]{2,1,0:T(8,128)(2,1)S(1)} %gather_fusion.13, pred[48]{0:T(512)(128)(4,1)S(1)} %get-tuple-element.10), kind=kOutput, calls=%fused_computation.86 | convolution fusion | flops 100859904 | bytes 7471152 | tf_op jit(solution)/shard_map/ltp,lpq->ltq/dot_general | solution.py:92
  244.6 1.0 convert_reduce_fusion
  246.9 19.3 %all_gather.29 = f32[16,8,16]{2,1,0:T(8,128)S(1)} all-gather(f32[1,8,16]{2,1,0:T(8,128)S(1)} %broadcast_select_fusion.6), channel_id=1, replica_groups=mesh['runs'=2,'area'=16] {'area'}, dimensions={0}, use_global_device_ids=true | all-gather | bytes 8704 | tf_op jit(solution)/shard_map/all_gather | solution.py:85
  267.2 3.6 %all-to-all-start.7 = ((bf16[16,3,16,256]{3,2,1,0:T(8,128)(2,1)}), bf16[16,3,16,256]{3,2,1,0:T(8,128)(2,1)S(1)}, u32[]{:S(2)}, u32[]{:S(2)}) async-start(bf16[16,3,16,256]{3,2,1,0:T(8,128)(2,1)} %bitcast.22), calls=%async_computation.7 | async-start | bytes 786432 | tf_op jit(solution)/shard_map/all_to_all | solution.py:78
  272.2 10.7 %all-to-all-done.7 = bf16[16,3,16,256]{3,2,1,0:T(8,128)(2,1)S(1)} async-done(((bf16[16,3,16,256]{3,2,1,0:T(8,128)(2,1)}), bf16[16,3,16,256]{3,2,1,0:T(8,128)(2,1)S(1)}, u32[]{:S(2)}, u32[]{:S(2)}) %all-to-all-start.7) | async-done | bytes 393248 | tf_op jit(solution)/shard_map/all_to_all | solution.py:78
  283.5 3.7 %fusion.60 = f32[48,16,256]{2,1,0:T(8,128)S(1)} fusion(bf16[48,256,256]{2,1,0:T(8,128)(2,1)} %param.29, bf16[48,16,256]{2,1,0:T(8,128)(2,1)S(1)} %gather_fusion.16, pred[48]{0:T(512)(128)(4,1)S(1)} %get-tuple-element.10), kind=kOutput, calls=%fused_computation.84 | convolution fusion | flops 100859904 | bytes 7471152 | tf_op jit(solution)/shard_map/ltp,lpq->ltq/dot_general | solution.py:92
  (113 shorter events, 38.4 us)
Async XLA Ops:
  0.0 58.2 %copy-start = (bf16[16,256,256]{2,1,0:T(8,128)(2,1)S(1)}, bf16[16,256,256]{2,1,0:T(8,128)(2,1)}, u32[]{:S(2)}) copy-start(bf16[16,256,256]{2,1,0:T(8,128)(2,1)} %param.33) | copy-start | bytes 6291460
  0.0 58.6 %copy-start.1 = (s32[16]{0:T(128)S(1)}, s32[16]{0:T(128)}, u32[]{:S(2)}) copy-start(s32[16]{0:T(128)} %param.31) | copy-start | bytes 196
  3.1 39.4 %all-to-all-start.1 = ((s32[16,1,3]{2,1,0:T(1,128)}), s32[16,1,3]{2,1,0:T(1,128)S(1)}, u32[]{:S(2)}, u32[]{:S(2)}) async-start(s32[16,1,3]{2,1,0:T(1,128)} %bitcast.6), calls=%async_computation.1 | async-start | bytes 16384 | tf_op jit(solution)/shard_map/all_to_all | solution.py:50
  42.5 9.9 %all-to-all-start = ((s32[16,1,3]{2,1,0:T(1,128)}), s32[16,1,3]{2,1,0:T(1,128)S(1)}, u32[]{:S(2)}, u32[]{:S(2)}) async-start(s32[16,1,3]{2,1,0:T(1,128)} %bitcast.5), calls=%async_computation | async-start | bytes 16384 | tf_op jit(solution)/shard_map/all_to_all | solution.py:53
  53.1 20.9 %copy-start.2 = (s32[48]{0:T(128)S(1)}, s32[48]{0:T(128)}, u32[]{:S(2)}) copy-start(s32[48]{0:T(128)} %param.27) | copy-start | bytes 580
  54.0 15.7 %all-to-all-start.2 = ((bf16[16,3,16,256]{3,2,1,0:T(8,128)(2,1)}), bf16[16,3,16,256]{3,2,1,0:T(8,128)(2,1)S(1)}, u32[]{:S(2)}, u32[]{:S(2)}) async-start(bf16[16,3,16,256]{3,2,1,0:T(8,128)(2,1)} %bitcast.8), calls=%async_computation.2 | async-start | bytes 786432 | tf_op jit(solution)/shard_map/all_to_all | solution.py:78
  96.6 15.7 %all-to-all-start.3 = ((bf16[16,3,16,256]{3,2,1,0:T(8,128)(2,1)}), bf16[16,3,16,256]{3,2,1,0:T(8,128)(2,1)S(1)}, u32[]{:S(2)}, u32[]{:S(2)}) async-start(bf16[16,3,16,256]{3,2,1,0:T(8,128)(2,1)} %bitcast.14), calls=%async_computation.3 | async-start | bytes 786432 | tf_op jit(solution)/shard_map/all_to_all | solution.py:78
  139.3 15.7 %all-to-all-start.4 = ((bf16[16,3,16,256]{3,2,1,0:T(8,128)(2,1)}), bf16[16,3,16,256]{3,2,1,0:T(8,128)(2,1)S(1)}, u32[]{:S(2)}, u32[]{:S(2)}) async-start(bf16[16,3,16,256]{3,2,1,0:T(8,128)(2,1)} %bitcast.16), calls=%async_computation.4 | async-start | bytes 786432 | tf_op jit(solution)/shard_map/all_to_all | solution.py:78
  181.9 15.7 %all-to-all-start.5 = ((bf16[16,3,16,256]{3,2,1,0:T(8,128)(2,1)}), bf16[16,3,16,256]{3,2,1,0:T(8,128)(2,1)S(1)}, u32[]{:S(2)}, u32[]{:S(2)}) async-start(bf16[16,3,16,256]{3,2,1,0:T(8,128)(2,1)} %bitcast.18), calls=%async_computation.5 | async-start | bytes 786432 | tf_op jit(solution)/shard_map/all_to_all | solution.py:78
  224.6 15.7 %all-to-all-start.6 = ((bf16[16,3,16,256]{3,2,1,0:T(8,128)(2,1)}), bf16[16,3,16,256]{3,2,1,0:T(8,128)(2,1)S(1)}, u32[]{:S(2)}, u32[]{:S(2)}) async-start(bf16[16,3,16,256]{3,2,1,0:T(8,128)(2,1)} %bitcast.20), calls=%async_computation.6 | async-start | bytes 786432 | tf_op jit(solution)/shard_map/all_to_all | solution.py:78
  267.2 15.7 %all-to-all-start.7 = ((bf16[16,3,16,256]{3,2,1,0:T(8,128)(2,1)}), bf16[16,3,16,256]{3,2,1,0:T(8,128)(2,1)S(1)}, u32[]{:S(2)}, u32[]{:S(2)}) async-start(bf16[16,3,16,256]{3,2,1,0:T(8,128)(2,1)} %bitcast.22), calls=%async_computation.7 | async-start | bytes 786432 | tf_op jit(solution)/shard_map/all_to_all | solution.py:78
